TPU v7x, 32 devices: a whole 2x2x4 slice. The times are simulated.
32 devices in a mesh: blk: 8 (over y, x, core), rep: 4 (over z).
Axes of the slice: x: 2, y: 2, z: 4, core: 2. Of those that a mesh axis runs over, the one named last changes fastest.
Arguments:
- embeddings: bfloat16 [8192, 512], P('blk'), may hold values from -1.5 to 1.5
- relation: float32 [4, 512], replicated, may hold values from 0.1 to 1.9
- head_ids: int32 [4, 8192], P(None, ('blk', 'rep')), may hold values from 0 to 1023
- context_ids: int32 [4, 8192], P(None, ('blk', 'rep')), may hold values from 0 to 1023
- neg_owner: int32 [4], replicated, may hold values from 0 to 7
- neg_ids: int32 [4, 768], replicated, may hold values from 0 to 1023
Outputs:
- embedding_grad: float32 [8192, 512], P('blk', 'rep')
All inputs are finite; a program needn't handle non-finite values.
Results may differ from a plain program's by a relative error of at most 0.0055.
Values may be sent and summed in bfloat16 or wider, within the bound.
A program may use at most 128 MiB of HBM per device.

v0:
```python
import jax
import jax.numpy as jnp
from jax import lax
from jax.sharding import PartitionSpec as P


def shifted(shard, axis, by):
    peers = lax.axis_size(axis)
    return lax.ppermute(shard, axis, [(i, (i + by) % peers) for i in range(peers)])


def broadcast(value, axis, source):
    kept = jnp.where(lax.axis_index(axis) == source, value, 0).astype(value.dtype)
    return lax.psum(kept, axis)


def stop_terms(home_rows, visitor, negatives, relation_row, head_index, context_index, weight):
    head_rows = jnp.take(home_rows, head_index, axis=0)
    context_rows = jnp.take(visitor, context_index, axis=0)
    weighted = (head_rows.astype(jnp.float32) * relation_row).astype(jnp.bfloat16)
    positive = jnp.sum(weighted.astype(jnp.float32) * context_rows.astype(jnp.float32), axis=1)
    scores = lax.dot_general(
        weighted, negatives, (((1,), (1,)), ((), ())), preferred_element_type=jnp.float32
    )
    pos_grad = -jax.nn.sigmoid(-positive)
    neg_grad = (weight * jax.nn.sigmoid(scores)).astype(jnp.bfloat16)
    pulled = jnp.dot(neg_grad, negatives, preferred_element_type=jnp.float32)
    head_terms = relation_row * (pos_grad[:, None] * context_rows.astype(jnp.float32) + pulled)
    context_terms = pos_grad[:, None] * weighted.astype(jnp.float32)
    empty = jnp.zeros((home_rows.shape[0], home_rows.shape[1]), jnp.float32)
    return (empty.at[head_index].add(head_terms), empty.at[context_index].add(context_terms))


def per_device(embeddings, relation, head_ids, context_ids, neg_owner, neg_ids):
    weight = 4.0 / neg_ids.shape[1]
    stop_count = head_ids.shape[0]
    visitor = embeddings
    head_total = jnp.zeros(embeddings.shape, jnp.float32)
    returned = jnp.zeros(embeddings.shape, jnp.float32)
    for stop_index in range(stop_count):
        visitor = shifted(visitor, "blk", 1)
        owner = neg_owner[stop_index]
        picked = jnp.take(embeddings, neg_ids[stop_index], axis=0)
        negatives = broadcast(picked, "blk", owner)
        head_part, context_part = stop_terms(
            embeddings,
            visitor,
            negatives,
            relation[stop_index],
            head_ids[stop_index],
            context_ids[stop_index],
            weight,
        )
        head_total = head_total + head_part
        returned = returned + shifted(
            context_part.astype(jnp.bfloat16), "blk", -(stop_index + 1)
        ).astype(context_part.dtype)
    combined = head_total + returned
    return lax.psum_scatter(combined, "rep", scatter_dimension=1, tiled=True)


def solution(mesh):
    in_specs = (P("blk", None), P(), P(None, ("blk", "rep")), P(None, ("blk", "rep")), P(), P())
    out_specs = P("blk", "rep")
    return jax.shard_map(
        per_device, mesh=mesh, in_specs=in_specs, out_specs=out_specs, check_vma=False
    )
```

profile of v0, /device:TPU:11, one launch (start us, length us, event | category | flops | bytes accessed | tf_op | source)
XLA Modules:
  0.0 241.2 jit_solution(7569741012426302793)
XLA Ops:
  6.5 1.8 collective-permute-start
  8.3 0.9 slice_reduce_fusion
  9.3 1.5 fusion.79
  13.3 0.0 copy-start
  13.3 4.8 %gather_fusion.8 = bf16[768,512]{1,0:T(8,128)(2,1)} fusion(bf16[1024,512]{1,0:T(8,128)(2,1)} %param.10, s32[1024]{0:T(1024)S(1)} %pad_clamp_fusion.3), kind=kCustom, calls=%fused_computation.10.clone | custom fusion | bytes 1575936 | tf_op jit(solution)/shard_map/jit(_take)/gather | solution.py:43
  18.1 3.3 %gather_fusion.2 = bf16[768,512]{1,0:T(8,128)(2,1)} fusion(bf16[1024,512]{1,0:T(8,128)(2,1)S(1)} %copy-done, s32[1024]{0:T(1024)S(1)} %pad_clamp_fusion.9), kind=kCustom, calls=%fused_computation.1.clone | custom fusion | bytes 1575936 | tf_op jit(solution)/shard_map/jit(_take)/gather | solution.py:43
  21.4 3.3 %gather_fusion.5 = bf16[768,512]{1,0:T(8,128)(2,1)} fusion(bf16[1024,512]{1,0:T(8,128)(2,1)S(1)} %copy-done, s32[1024]{0:T(1024)S(1)} %pad_clamp_fusion.6), kind=kCustom, calls=%fused_computation.9.clone | custom fusion | bytes 1575936 | tf_op jit(solution)/shard_map/jit(_take)/gather | solution.py:43
  24.8 2.7 %gather_fusion.11 = bf16[768,512]{1,0:T(8,128)(2,1)S(1)} fusion(bf16[1024,512]{1,0:T(8,128)(2,1)S(1)} %copy-done, s32[1024]{0:T(1024)S(1)} %pad_clamp_fusion), kind=kCustom, calls=%fused_computation.11.clone | custom fusion | bytes 1575936 | tf_op jit(solution)/shard_map/jit(_take)/gather | solution.py:43
  27.5 0.0 copy-start.2
  27.5 0.0 copy-start.1
  27.5 2.3 select_select_fusion.1
  29.8 1.0 select_select_fusion.3
  30.8 1.1 select_select_fusion.2
  31.9 1.1 select_select_fusion
  33.0 0.0 all-reduce.3.cloned.1.call-update
  33.0 0.0 reduce-scatter.2.cloned.1.call-start
  33.2 0.0 collective-permute-done
  33.2 0.1 collective-permute-start.1
  33.4 24.4 %collective-permute-done.1 = bf16[1024,512]{1,0:T(8,128)(2,1)} collective-permute-done((bf16[1024,512]{1,0:T(8,128)(2,1)S(1)}, bf16[1024,512]{1,0:T(8,128)(2,1)}, u32[]{:S(2)}, u32[]{:S(2)}) %collective-permute-start.1) | collective-permute-done | bytes 1048608 | tf_op jit(solution)/shard_map/ppermute | solution.py:9
  57.8 3.5 %collective-permute-start.2 = (bf16[1024,512]{1,0:T(8,128)(2,1)}, bf16[1024,512]{1,0:T(8,128)(2,1)S(1)}, u32[]{:S(2)}, u32[]{:S(2)}) collective-permute-start(bf16[1024,512]{1,0:T(8,128)(2,1)} %collective-permute-done.1), channel_id=1, source_target_pairs={{0,4},{4,8},{8,12},{12,16},{16,20},{20,24},{24,28},{28,0},{1,5},{5... | collective-permute-start | bytes 3145736 | tf_op jit(solution)/shard_map/ppermute | solution.py:9
  61.3 1.9 gather_fusion.9
  63.1 1.8 gather_fusion.3
  65.0 1.9 gather_fusion
  66.9 1.2 gather_fusion.6
  68.1 1.2 gather_fusion.1
  69.3 8.3 %collective-permute-done.2 = bf16[1024,512]{1,0:T(8,128)(2,1)S(1)} collective-permute-done((bf16[1024,512]{1,0:T(8,128)(2,1)}, bf16[1024,512]{1,0:T(8,128)(2,1)S(1)}, u32[]{:S(2)}, u32[]{:S(2)}) %collective-permute-start.2) | collective-permute-done | bytes 1048608 | tf_op jit(solution)/shard_map/ppermute | solution.py:9
  77.6 3.3 %collective-permute-start.3 = (bf16[1024,512]{1,0:T(8,128)(2,1)S(1)}, bf16[1024,512]{1,0:T(8,128)(2,1)}, u32[]{:S(2)}, u32[]{:S(2)}) collective-permute-start(bf16[1024,512]{1,0:T(8,128)(2,1)S(1)} %collective-permute-done.2), channel_id=1, source_target_pairs={{0,4},{4,8},{8,12},{12,16},{16,20},{20,24},{24,28},{28,0},{1,5},{5... | collective-permute-start | bytes 3145736 | tf_op jit(solution)/shard_map/ppermute | solution.py:9
  80.8 0.3 fusion.41
  81.1 3.2 %scatter_custom_fusion.2 = f32[1024,512]{1,0:T(8,128)S(1)} fusion(s32[256]{0:T(256)S(1)} %bitcast.78, f32[]{:T(128)} %constant.24.clone.1, f32[256]{0:T(256)S(1)} %divide_negate_fusion.3, bf16[256,512]{1,0:T(8,128)(2,1)} %gather_fusion, f32[512]{0:T(512)S(1)} %bitcast.56, pred[256]{0:T(512)(128)(4,1)S(1)} %get-tuple-element.44), kind=kCustom, calls=%fused_computation.59 | custom fusion | flops 917504 | bytes 2362884 | tf_op jit(solution)/shard_map/scatter-add | solution.py:31
  84.3 1.1 convert_element_type.117
  85.4 0.0 collective-permute-start.4
  85.4 2.6 %gather_fusion.4 = bf16[256,512]{1,0:T(8,128)(2,1)S(1)} fusion(bf16[1024,512]{1,0:T(8,128)(2,1)} %collective-permute-done.1, s32[1024]{0:T(1024)S(1)} %pad_clamp_fusion.7), kind=kCustom, calls=%fused_computation.4.clone | custom fusion | bytes 525312 | tf_op jit(solution)/shard_map/jit(_take)/gather | solution.py:19
  88.0 0.3 fusion.44
  88.3 0.4 copy-done.11
  88.7 3.1 %scatter_custom_fusion.3 = f32[1024,512]{1,0:T(8,128)S(1)} fusion(s32[256]{0:T(256)S(1)} %bitcast.77, f32[]{:T(128)} %constant.24.clone.1, f32[256]{0:T(256)S(1)} %divide_negate_fusion.2, bf16[256,512]{1,0:T(8,128)(2,1)} %gather_fusion.3, f32[512]{0:T(512)S(1)} %bitcast.53, pred[256]{0:T(512)(128)(4,1)S(1)} %get-tuple-element.42), kind=kCustom, calls=%fused_computation.57 | custom fusion | flops 917504 | bytes 2362884 | tf_op jit(solution)/shard_map/scatter-add | solution.py:31
  91.9 1.2 convert_element_type.119
  93.1 0.0 collective-permute-start.5
  93.1 1.2 gather_fusion.7
  94.2 0.3 fusion.47
  94.5 0.4 copy-done.13
  94.9 2.7 %scatter_custom_fusion.4 = f32[1024,512]{1,0:T(8,128)S(1)} fusion(s32[256]{0:T(256)S(1)} %bitcast.76, f32[]{:T(128)} %constant.24.clone.1, f32[256]{0:T(256)S(1)} %divide_negate_fusion.1, bf16[256,512]{1,0:T(8,128)(2,1)S(1)} %gather_fusion.6, f32[512]{0:T(512)S(1)} %bitcast.50, pred[256]{0:T(512)(128)(4,1)S(1)} %get-tuple-element.40), kind=kCustom, calls=%fused_computation.55 | custom fusion | flops 917504 | bytes 2362884 | tf_op jit(solution)/shard_map/scatter-add | solution.py:31
  97.6 1.1 convert_element_type.121
  98.7 1.4 collective-permute-start.6
  100.2 11.8 %collective-permute-done.3 = bf16[1024,512]{1,0:T(8,128)(2,1)} collective-permute-done((bf16[1024,512]{1,0:T(8,128)(2,1)S(1)}, bf16[1024,512]{1,0:T(8,128)(2,1)}, u32[]{:S(2)}, u32[]{:S(2)}) %collective-permute-start.3) | collective-permute-done | bytes 1048608 | tf_op jit(solution)/shard_map/ppermute | solution.py:9
  112.0 2.6 %gather_fusion.10 = bf16[256,512]{1,0:T(8,128)(2,1)S(1)} fusion(bf16[1024,512]{1,0:T(8,128)(2,1)} %collective-permute-done.3, s32[1024]{0:T(1024)S(1)} %pad_clamp_fusion.1), kind=kCustom, calls=%fused_computation.8.clone | custom fusion | bytes 525312 | tf_op jit(solution)/shard_map/jit(_take)/gather | solution.py:19
  114.6 0.3 fusion.50
  114.9 3.4 %scatter_custom_fusion.5 = f32[1024,512]{1,0:T(8,128)S(1)} fusion(s32[256]{0:T(256)S(1)} %bitcast.75, f32[]{:T(128)} %constant.24.clone.1, f32[256]{0:T(256)S(1)} %divide_negate_fusion, bf16[256,512]{1,0:T(8,128)(2,1)} %gather_fusion.9, f32[512]{0:T(512)S(1)} %bitcast.46, pred[256]{0:T(512)(128)(4,1)S(1)} %compare_and_fusion.5), kind=kCustom, calls=%fused_computation.53 | custom fusion | flops 917504 | bytes 2362884 | tf_op jit(solution)/shard_map/scatter-add | solution.py:31
  118.2 0.0 copy-start.6
  118.2 1.2 convert_element_type.123
  119.4 0.0 collective-permute-start.7
  119.4 43.1 %all-reduce.3.cloned.1.call-done = (bf16[768,512]{1,0:T(8,128)(2,1)}, bf16[768,512]{1,0:T(8,128)(2,1)}, bf16[768,512]{1,0:T(8,128)(2,1)}, bf16[768,512]{1,0:T(8,128)(2,1)}) async-done(((bf16[768,512]{1,0:T(8,128)(2,1)}, bf16[768,512]{1,0:T(8,128)(2,1)}, bf16[768,512]{1,0:T(8,128)(2,1)}, bf16[768,512]{1,0:T(8,128)(2,1)}), (bf16[768,512]{1,0:T(8,128)(2,1)}, bf16[768,512]{1,0:T(8,128)(2,1)}, ...) | async-done | bytes 3145744 | tf_op jit(solution)/shard_map/psum | solution.py:14
  162.6 3.0 %fusion.29 = f32[256,512]{1,0:T(8,128)} fusion(bf16[768,512]{1,0:T(8,128)(2,1)} %get-tuple-element.14, bf16[256,512]{1,0:T(8,128)(2,1)S(1)} %copy-done.6, f32[512]{0:T(512)S(1)} %bitcast.47, pred[256]{0:T(512)(128)(4,1)S(1)} %compare_and_fusion.5), kind=kOutput, calls=%fused_computation.52 | convolution fusion | flops 404160512 | bytes 1575168 | tf_op jit(solution)/shard_map/dot_general | solution.py:27
  165.6 1.6 fusion.43
  167.1 1.5 fusion.46
  168.7 1.5 fusion.49
  170.2 8.1 %scatter_custom_fusion = f32[1024,512]{1,0:T(8,128)S(1)} fusion(s32[768]{0:T(1024)S(1)} %add_reduce_fusion, f32[256,512]{1,0:T(8,128)} %fusion.49, f32[]{:T(128)} %constant.46, f32[256,512]{1,0:T(8,128)} %fusion.46, f32[256,512]{1,0:T(8,128)} %fusion.43, f32[]{:T(128)} %constant.24.clone.1), kind=kCustom, calls=%fused_computation.19 | custom fusion | flops 1179648 | bytes 3670024 | tf_op jit(solution)/shard_map/add | solution.py:54
  178.3 3.6 %scatter_custom_fusion.1 = f32[1024,512]{1,0:T(8,128)} fusion(s32[256]{0:T(256)S(1)} %bitcast.74, f32[]{:T(128)} %constant.24.clone.1, f32[256,512]{1,0:T(8,128)S(1)} %copy-done.15, f32[256]{0:T(256)S(1)} %divide_negate_fusion, f32[512]{0:T(512)S(1)} %bitcast.48, bf16[256,512]{1,0:T(8,128)(2,1)S(1)} %gather_fusion.10, ...), kind=kCustom, calls=%fused_computation.61 | custom fusion | flops 786432 | bytes 2887174 | tf_op jit(solution)/shard_map/scatter-add | solution.py:31
  181.9 0.0 collective-permute-done.4
  182.0 0.0 collective-permute-done.5
  182.0 0.0 collective-permute-done.6
  182.0 0.0 collective-permute-done.7
  182.0 5.0 %add_add_fusion = f32[1024,512]{1,0:T(8,128)} fusion(bf16[1024,512]{1,0:T(8,128)(2,1)} %collective-permute-done.7, bf16[1024,512]{1,0:T(8,128)(2,1)} %collective-permute-done.6, bf16[1024,512]{1,0:T(8,128)(2,1)} %collective-permute-done.5, bf16[1024,512]{1,0:T(8,128)(2,1)} %collective-permute-done.4, f32[1024,512]{1,0:T(8,128)S(1)} %scatter_custom_fusion, ...), kind=kLoop, calls=%fused_computation.18 | loop fusion | flops 4718592 | bytes 10485760 | tf_op jit(solution)/shard_map/add | solution.py:58
  187.0 0.0 reduce-scatter.2.cloned.1.call-update
  187.0 47.3 %reduce-scatter.2.cloned.1.call-done = f32[1024,128]{1,0:T(8,128)} async-done(((f32[1024,512]{1,0:T(8,128)}), f32[1024,128]{1,0:T(8,128)}) %reduce-scatter.2.cloned.1.call-update) | async-done | bytes 524304 | tf_op jit(solution)/shard_map/reduce_scatter | solution.py:59
  (78 shorter events, 0.3 us)
Async XLA Ops:
  6.5 156.0 %all-reduce.3.cloned.1.call-start = ((), (), s32[]{:S(2)}) async-start(), calls=%async_computation.2 | async-start | bytes 6291456 | tf_op jit(solution)/shard_map/psum | solution.py:14
  6.5 26.7 %collective-permute-start = (bf16[1024,512]{1,0:T(8,128)(2,1)}, bf16[1024,512]{1,0:T(8,128)(2,1)S(1)}, u32[]{:S(2)}, u32[]{:S(2)}) collective-permute-start(bf16[1024,512]{1,0:T(8,128)(2,1)} %param.10), channel_id=1, source_target_pairs={{0,4},{4,8},{8,12},{12,16},{16,20},{20,24},{24,28},{28,0},{1,5},{5... | collective-permute-start | bytes 3145736 | tf_op jit(solution)/shard_map/ppermute | solution.py:9
  13.3 4.8 %copy-start = (bf16[1024,512]{1,0:T(8,128)(2,1)S(1)}, bf16[1024,512]{1,0:T(8,128)(2,1)}, u32[]{:S(2)}) copy-start(bf16[1024,512]{1,0:T(8,128)(2,1)} %param.10) | copy-start | bytes 3145732
  27.5 2.3 copy-start.2
  27.5 3.4 %copy-start.1 = (bf16[768,512]{1,0:T(8,128)(2,1)S(1)}, bf16[768,512]{1,0:T(8,128)(2,1)}, u32[]{:S(2)}) copy-start(bf16[768,512]{1,0:T(8,128)(2,1)} %gather_fusion.5) | copy-start | bytes 2359300
  31.9 1.1 copy-start.16
  31.9 1.3 copy-start.17
  33.0 201.3 %reduce-scatter.2.cloned.1.call-start = ((), (), s32[]{:S(2)}) async-start(), calls=%async_computation.1 | async-start | bytes 2621440 | tf_op jit(solution)/shard_map/reduce_scatter | solution.py:59
  33.2 24.6 %collective-permute-start.1 = (bf16[1024,512]{1,0:T(8,128)(2,1)S(1)}, bf16[1024,512]{1,0:T(8,128)(2,1)}, u32[]{:S(2)}, u32[]{:S(2)}) collective-permute-start(bf16[1024,512]{1,0:T(8,128)(2,1)S(1)} %collective-permute-done), channel_id=1, source_target_pairs={{0,4},{4,8},{8,12},{12,16},{16,20},{20,24},{24,28},{28,0},{1,5},{5... | collective-permute-start | bytes 3145736 | tf_op jit(solution)/shard_map/ppermute | solution.py:9
  57.8 19.8 %collective-permute-start.2 = (bf16[1024,512]{1,0:T(8,128)(2,1)}, bf16[1024,512]{1,0:T(8,128)(2,1)S(1)}, u32[]{:S(2)}, u32[]{:S(2)}) collective-permute-start(bf16[1024,512]{1,0:T(8,128)(2,1)} %collective-permute-done.1), channel_id=1, source_target_pairs={{0,4},{4,8},{8,12},{12,16},{16,20},{20,24},{24,28},{28,0},{1,5},{5... | collective-permute-start | bytes 3145736 | tf_op jit(solution)/shard_map/ppermute | solution.py:9
  65.0 3.1 %copy-start.18 = (f32[4,512]{1,0:T(4,128)S(1)}, f32[4,512]{1,0:T(4,128)}, u32[]{:S(2)}) copy-start(f32[4,512]{1,0:T(4,128)} %param.11) | copy-start | bytes 24580
  68.0 12.8 %copy-start.7 = (bf16[256,512]{1,0:T(8,128)(2,1)S(1)}, bf16[256,512]{1,0:T(8,128)(2,1)}, u32[]{:S(2)}) copy-start(bf16[256,512]{1,0:T(8,128)(2,1)} %gather_fusion) | copy-start | bytes 786436
  69.3 11.8 %copy-start.9 = (bf16[256,512]{1,0:T(8,128)(2,1)}, bf16[256,512]{1,0:T(8,128)(2,1)S(1)}, u32[]{:S(2)}) copy-start(bf16[256,512]{1,0:T(8,128)(2,1)S(1)} %gather_fusion.1) | copy-start | bytes 786436
  77.6 34.4 %collective-permute-start.3 = (bf16[1024,512]{1,0:T(8,128)(2,1)S(1)}, bf16[1024,512]{1,0:T(8,128)(2,1)}, u32[]{:S(2)}, u32[]{:S(2)}) collective-permute-start(bf16[1024,512]{1,0:T(8,128)(2,1)S(1)} %collective-permute-done.2), channel_id=1, source_target_pairs={{0,4},{4,8},{8,12},{12,16},{16,20},{20,24},{24,28},{28,0},{1,5},{5... | collective-permute-start | bytes 3145736 | tf_op jit(solution)/shard_map/ppermute | solution.py:9
  85.4 2.6 %copy-start.3 = (bf16[256,512]{1,0:T(8,128)(2,1)S(1)}, bf16[256,512]{1,0:T(8,128)(2,1)}, u32[]{:S(2)}) copy-start(bf16[256,512]{1,0:T(8,128)(2,1)} %gather_fusion.3) | copy-start | bytes 786436
  85.4 96.5 %collective-permute-start.4 = (bf16[1024,512]{1,0:T(8,128)(2,1)}, bf16[1024,512]{1,0:T(8,128)(2,1)}, u32[]{:S(2)}, u32[]{:S(2)}) collective-permute-start(bf16[1024,512]{1,0:T(8,128)(2,1)} %convert_element_type.117), channel_id=1, source_target_pairs={{0,28},{4,0},{8,4},{12,8},{16,12},{20,16},{24,20},{28,24},{1,29},{... | collective-permute-start | bytes 3145736 | tf_op jit(solution)/shard_map/ppermute | solution.py:9
  88.0 0.7 copy-start.11
  93.1 88.9 %collective-permute-start.5 = (bf16[1024,512]{1,0:T(8,128)(2,1)}, bf16[1024,512]{1,0:T(8,128)(2,1)}, u32[]{:S(2)}, u32[]{:S(2)}) collective-permute-start(bf16[1024,512]{1,0:T(8,128)(2,1)} %convert_element_type.119), channel_id=1, source_target_pairs={{0,24},{4,28},{8,0},{12,4},{16,8},{20,12},{24,16},{28,20},{1,25},{... | collective-permute-start | bytes 3145736 | tf_op jit(solution)/shard_map/ppermute | solution.py:9
  94.2 0.7 copy-start.13
  98.7 15.8 %copy-start.5 = (bf16[256,512]{1,0:T(8,128)(2,1)S(1)}, bf16[256,512]{1,0:T(8,128)(2,1)}, u32[]{:S(2)}) copy-start(bf16[256,512]{1,0:T(8,128)(2,1)} %gather_fusion.9) | copy-start | bytes 786436
  98.7 83.2 %collective-permute-start.6 = (bf16[1024,512]{1,0:T(8,128)(2,1)}, bf16[1024,512]{1,0:T(8,128)(2,1)}, u32[]{:S(2)}, u32[]{:S(2)}) collective-permute-start(bf16[1024,512]{1,0:T(8,128)(2,1)} %convert_element_type.121), channel_id=1, source_target_pairs={{0,20},{4,24},{8,28},{12,0},{16,4},{20,8},{24,12},{28,16},{1,21},{... | collective-permute-start | bytes 3145736 | tf_op jit(solution)/shard_map/ppermute | solution.py:9
  118.2 44.3 %copy-start.6 = (bf16[256,512]{1,0:T(8,128)(2,1)S(1)}, bf16[256,512]{1,0:T(8,128)(2,1)}, u32[]{:S(2)}) copy-start(bf16[256,512]{1,0:T(8,128)(2,1)} %gather_fusion.9) | copy-start | bytes 786436
  119.4 62.6 %collective-permute-start.7 = (bf16[1024,512]{1,0:T(8,128)(2,1)}, bf16[1024,512]{1,0:T(8,128)(2,1)}, u32[]{:S(2)}, u32[]{:S(2)}) collective-permute-start(bf16[1024,512]{1,0:T(8,128)(2,1)} %convert_element_type.123), channel_id=1, source_target_pairs={{0,16},{4,20},{8,24},{12,28},{16,0},{20,4},{24,8},{28,12},{1,17},{... | collective-permute-start | bytes 3145736 | tf_op jit(solution)/shard_map/ppermute | solution.py:9
  162.5 3.0 %copy-start.8 = (bf16[256,512]{1,0:T(8,128)(2,1)S(1)}, bf16[256,512]{1,0:T(8,128)(2,1)}, u32[]{:S(2)}) copy-start(bf16[256,512]{1,0:T(8,128)(2,1)} %gather_fusion) | copy-start | bytes 786436
  162.6 3.0 %copy-start.10 = (bf16[256,512]{1,0:T(8,128)(2,1)S(1)}, bf16[256,512]{1,0:T(8,128)(2,1)}, u32[]{:S(2)}) copy-start(bf16[256,512]{1,0:T(8,128)(2,1)} %copy-done.9) | copy-start | bytes 786436
  162.6 3.0 %copy-start.21 = (bf16[768,512]{1,0:T(8,128)(2,1)S(1)}, bf16[768,512]{1,0:T(8,128)(2,1)}, u32[]{:S(2)}) copy-start(bf16[768,512]{1,0:T(8,128)(2,1)} %get-tuple-element.13) | copy-start | bytes 2359300
  165.5 1.6 copy-start.4
  165.5 1.6 copy-start.12
  165.6 1.6 copy-start.20
  167.1 1.5 copy-start.14
  167.1 1.5 copy-start.19
  170.2 8.1 %copy-start.15 = (f32[256,512]{1,0:T(8,128)S(1)}, f32[256,512]{1,0:T(8,128)}, u32[]{:S(2)}) copy-start(f32[256,512]{1,0:T(8,128)} %fusion.29) | copy-start | bytes 1572868
Sparse Core Ops, SparseCore 0:
  33.1 129.3 all-reduce.2
  187.1 47.1 reduce-scatter.1
where the time goes:
time: 246 us; the launch traced here: 241 us
  waiting for transfers between devices  135 us (55%)
  other arithmetic  40.5 us (16%)
  local copies, waits for them, and re-layouts  31.6 us (13%)
  between operations  16.5 us (7%)
  starting transfers between devices  10.1 us (4%)
  matrix products  7.54 us (3%)
    reduce_scatter x1, waiting for transfers between devices, per_device(): return lax.psum_scatter(combined, 'rep', scatter_dimension=1, tiled=True)  47.3 us
    ppermute x8, waiting for transfers between devices, shifted(): lax.ppermute(shard, axis, [(i, (i + by) % peers) for i in range(peers)])  44.5 us
    psum x1, waiting for transfers between devices, broadcast(): return lax.psum(kept, axis)  43.1 us
    gather x4, local copies, waits for them, and re-layouts, per_device(): picked = jnp.take(embeddings, neg_ids[stop_index], axis=0)  14.1 us
    scatter-add x4, other arithmetic, stop_terms(): empty.at[context_index].add(context_terms)  12.4 us
    ppermute x8, starting transfers between devices, shifted(): lax.ppermute(shard, axis, [(i, (i + by) % peers) for i in range(peers)])  10 us
    add x1, other arithmetic, per_device(): head_total = head_total + head_part  8.12 us
    dot_general x4, matrix products, stop_terms(): pulled = jnp.dot(neg_grad, negatives, preferred_element_type=jnp.float32)  7.54 us
  transfers between devices with their start and end apart: 10, of which 5 were waited for; matrix products, arithmetic and copies ran while one was open for 31% of the time, Pallas kernels for 0%

commit v1 on v0

--- a/solution.py
+++ b/solution.py
@@ -1,7 +1,281 @@
+import functools
+
 import jax
 import jax.numpy as jnp
 from jax import lax
+from jax.experimental import pallas as pl
+from jax.experimental.pallas import tpu as pltpu
 from jax.sharding import PartitionSpec as P
+
+MESH = pl.DeviceIdType.MESH
+F32 = jnp.float32
+BF16 = jnp.bfloat16
+
+
+def column_of(row):
+    wide = jnp.broadcast_to(row.astype(F32), (8, row.shape[1]))
+    return jnp.transpose(wide)[:, :1]
+
+
+def by_edge(row, rows):
+    column = column_of(row)
+    lanes = lax.broadcasted_iota(jnp.int32, (row.shape[1], rows), 1).astype(F32)
+    return jnp.where(column == lanes, 1.0, 0.0).astype(BF16)
+
+
+def by_entity(row, rows, value):
+    sublanes = lax.broadcasted_iota(jnp.int32, (rows, row.shape[1]), 0)
+    return jnp.where(row == sublanes, value, 0.0).astype(BF16)
+
+
+def kernel(
+    n_blk, n_rep, weight,
+    owner_ref, emb_ref, rel_ref, ids_ref, neg_ids_ref, out_ref,
+    parts, idz, idn, mine, his, ctx, part_dot, pos_grad, pos_in, neg_cut, neg, pulled, spread, give, take,
+    wide, rel_cols, rel_stop, ag_send, ag_recv, fw_send, fw_recv, idz_send, idz_recv, idn_send, idn_recv,
+    dot_send, dot_recv, pg_send, pg_recv, neg_send, neg_recv, sib_send, sib_recv, rs_send, rs_recv,
+):
+    b, z = lax.axis_index("blk"), lax.axis_index("rep")
+    rows = emb_ref.shape[0]
+    stops = rel_ref.shape[0]
+    edges = ids_ref.shape[1]
+    width = out_ref.shape[1]
+    negs = neg_ids_ref.shape[1]
+    half = negs // 2
+    core = lax.rem(b, 2)
+    sibling = b + 1 - 2 * core
+    cols = pl.ds(pl.multiple_of(z * width, width), width)
+
+    def plane(j):
+        return lax.rem(b + j + n_blk, n_blk)
+
+    def column_peer(j):
+        return lax.rem(z + j + n_rep, n_rep)
+
+    def remote(src, dst, send, recv, at_blk, at_rep):
+        return pltpu.make_async_remote_copy(
+            src_ref=src, dst_ref=dst, send_sem=send, recv_sem=recv,
+            device_id=(at_blk, at_rep), device_id_type=MESH,
+        )
+
+    barrier = pltpu.get_barrier_semaphore()
+    for j in range(1, n_blk):
+        pl.semaphore_signal(barrier, inc=1, device_id=(plane(j), z), device_id_type=MESH)
+    for j in range(1, n_rep):
+        pl.semaphore_signal(barrier, inc=1, device_id=(b, column_peer(j)), device_id_type=MESH)
+    parts[b] = emb_ref[:, cols]
+    rel_cols[...] = rel_ref[:, cols]
+    own_relation = rel_ref[pl.ds(z, 1), :]
+    for r in range(n_rep):
+        rel_stop[r] = own_relation[:, r * width : (r + 1) * width]
+    idz[z] = ids_ref[...]
+    pl.semaphore_wait(barrier, n_blk - 1 + n_rep - 1)
+
+    idz_copies = [
+        remote(idz.at[z], idz.at[z], idz_send.at[j], idz_recv.at[j], b, column_peer(j))
+        for j in range(1, n_rep)
+    ]
+    for copy in idz_copies:
+        copy.start()
+    jumps = list(range(2, n_blk, 2))
+    ag_copies = [
+        remote(parts.at[b], parts.at[b], ag_send.at[i], ag_recv.at[i], plane(j), z)
+        for i, j in enumerate(jumps)
+    ]
+    for copy in ag_copies:
+        copy.start()
+    own_fw = remote(parts.at[b], parts.at[b], fw_send.at[len(jumps)], fw_recv.at[len(jumps)], sibling, z)
+    own_fw.start()
+    for copy in idz_copies:
+        copy.wait()
+    idn_copies = [
+        remote(idz, idn.at[k - 1], idn_send.at[k - 1], idn_recv.at[k - 1], plane(-k), z)
+        for k in range(1, stops + 1)
+    ]
+    for copy in idn_copies:
+        copy.start()
+
+    def gather_home(t, carry):
+        s, r = t // n_rep, lax.rem(t, n_rep)
+        hot = by_edge(idz[r, pl.ds(s, 1), :], rows)
+        picked = jnp.dot(hot, parts[b], preferred_element_type=F32)
+        mine[t] = (picked * rel_cols[pl.ds(s, 1), :]).astype(BF16)
+        return carry
+
+    def gather_wide(r, carry):
+        hot = by_edge(idz[r, pl.ds(z, 1), :], rows)
+        picked = jnp.dot(hot, emb_ref[...], preferred_element_type=F32)
+        wide[r] = (picked * rel_ref[pl.ds(z, 1), :]).astype(BF16)
+        return carry
+
+    lax.fori_loop(0, n_rep, gather_wide, 0)
+
+    fw_copies = []
+    for i, j in enumerate(jumps):
+        ag_copies[i].wait()
+        source = plane(-j)
+        copy = remote(parts.at[source], parts.at[source], fw_send.at[i], fw_recv.at[i], sibling, z)
+        copy.start()
+        fw_copies.append(copy)
+    lax.fori_loop(0, stops * n_rep, gather_home, 0)
+    for copy in fw_copies + [own_fw]:
+        copy.wait()
+
+    lower = pl.ds(pl.multiple_of(core * half, half), half)
+    for s in range(stops):
+        ids_row = jnp.where(core == 0, neg_ids_ref[s : s + 1, :half], neg_ids_ref[s : s + 1, half:])
+        hot = by_edge(ids_row, rows)
+        neg_cut[s] = jnp.dot(hot, parts[owner_ref[s]], preferred_element_type=F32).astype(BF16)
+    neg_copies = [
+        remote(neg_cut.at[column_peer(j)], neg.at[lower, cols], neg_send.at[j], neg_recv.at[j], b, column_peer(j))
+        for j in range(1, n_rep)
+    ]
+    for copy in neg_copies:
+        copy.start()
+    neg[lower, cols] = neg_cut[z]
+
+    def gather_context(t, carry):
+        s, r = t // n_rep, lax.rem(t, n_rep)
+        hot = by_edge(idz[r, pl.ds(stops + s, 1), :], rows)
+        rows_in = jnp.dot(hot, parts[lax.rem(b - s - 1 + n_blk, n_blk)], preferred_element_type=F32)
+        ctx[t] = rows_in.astype(BF16)
+        product = mine[t].astype(F32) * rows_in
+        part_dot[z, pl.ds(t, 1), :] = jnp.sum(jnp.transpose(product), axis=0, keepdims=True)
+        return carry
+
+    lax.fori_loop(0, stops * n_rep, gather_context, 0)
+    dot_copies = [
+        remote(part_dot.at[z], part_dot.at[z], dot_send.at[j], dot_recv.at[j], b, column_peer(j))
+        for j in range(1, n_rep)
+    ]
+    for copy in dot_copies:
+        copy.start()
+
+    for copy in idn_copies:
+        copy.wait()
+
+    def gather_incoming(t, carry):
+        s, r = t // n_rep, lax.rem(t, n_rep)
+        hot = by_edge(idn[s, r, pl.ds(s, 1), :], rows)
+        picked = jnp.dot(hot, parts[lax.rem(b + s + 1, n_blk)], preferred_element_type=F32)
+        his[t] = (picked * rel_cols[pl.ds(s, 1), :]).astype(BF16)
+        return carry
+
+    for copy in neg_copies:
+        copy.wait()
+    sib_copy = remote(neg.at[lower, :], neg.at[lower, :], sib_send, sib_recv, sibling, z)
+    sib_copy.start()
+    for copy in dot_copies:
+        copy.wait()
+    positive = part_dot[0]
+    for r in range(1, n_rep):
+        positive = positive + part_dot[r]
+    pos_grad[...] = -jax.nn.sigmoid(-positive)
+    pg_copies = [
+        remote(pos_grad, pos_in.at[k - 1], pg_send.at[k - 1], pg_recv.at[k - 1], plane(-k), z)
+        for k in range(1, stops + 1)
+    ]
+    for copy in pg_copies:
+        copy.start()
+    sib_copy.wait()
+
+    def negatives(r, carry):
+        scores = lax.dot_general(
+            wide[r], neg[...], (((1,), (1,)), ((), ())), preferred_element_type=F32
+        )
+        neg_grad = (weight * jax.nn.sigmoid(scores)).astype(BF16)
+        at = pl.ds(pl.multiple_of(r * edges, edges), edges)
+        pulled[at, :] = jnp.dot(neg_grad, neg[...], preferred_element_type=F32).astype(BF16)
+        spread[:, at] = by_entity(idz[r, pl.ds(z, 1), :], rows, 1.0)
+        return carry
+
+    lax.fori_loop(0, n_rep, negatives, 0)
+    rs_copies = []
+    for j in list(range(1, n_rep)) + [0]:
+        to = column_peer(j)
+        there = pl.ds(pl.multiple_of(to * width, width), width)
+        summed = jnp.dot(spread[...], pulled[:, there], preferred_element_type=F32)
+        summed = summed * rel_stop[to]
+        if j == 0:
+            out_ref[...] = summed
+        else:
+            give[j - 1] = summed.astype(BF16)
+            copy = remote(give.at[j - 1], take.at[j - 1], rs_send.at[j], rs_recv.at[j], b, to)
+            copy.start()
+            rs_copies.append(copy)
+    lax.fori_loop(0, stops * n_rep, gather_incoming, 0)
+
+    def scatter_home(s, carry):
+        total = jnp.zeros((rows, width), F32)
+        for r in range(n_rep):
+            t = s * n_rep + r
+            hot = by_entity(idz[r, pl.ds(s, 1), :], rows, pos_grad[pl.ds(t, 1), :])
+            total = total + jnp.dot(hot, ctx[t], preferred_element_type=F32)
+        out_ref[...] += total * rel_cols[pl.ds(s, 1), :]
+        return carry
+
+    lax.fori_loop(0, stops, scatter_home, 0)
+    for copy in pg_copies:
+        copy.wait()
+
+    def scatter_incoming(s, carry):
+        total = jnp.zeros((rows, width), F32)
+        for r in range(n_rep):
+            t = s * n_rep + r
+            hot = by_entity(idn[s, r, pl.ds(stops + s, 1), :], rows, pos_in[s, pl.ds(t, 1), :])
+            total = total + jnp.dot(hot, his[t], preferred_element_type=F32)
+        out_ref[...] += total
+        return carry
+
+    lax.fori_loop(0, stops, scatter_incoming, 0)
+    for copy in rs_copies:
+        copy.wait()
+    for j in range(n_rep - 1):
+        out_ref[...] += take[j].astype(F32)
+
+
+def fused(n_blk, n_rep, embeddings, relation, head_ids, context_ids, neg_owner, neg_ids):
+    rows, dim = embeddings.shape
+    stops, edges = head_ids.shape
+    negs = neg_ids.shape[1]
+    width = dim // n_rep
+    ids = jnp.concatenate([head_ids, context_ids], axis=0)
+    blocks = stops * n_rep
+    vmem = pl.BlockSpec(memory_space=pltpu.VMEM)
+    dma = pltpu.SemaphoreType.DMA
+    return pl.pallas_call(
+        functools.partial(kernel, n_blk, n_rep, 4.0 / negs),
+        out_shape=jax.ShapeDtypeStruct((rows, width), F32),
+        in_specs=[pl.BlockSpec(memory_space=pltpu.SMEM)] + [vmem] * 4,
+        out_specs=vmem,
+        scratch_shapes=[
+            pltpu.VMEM((n_blk, rows, width), BF16),
+            pltpu.VMEM((n_rep, 2 * stops, edges), jnp.int32),
+            pltpu.VMEM((stops, n_rep, 2 * stops, edges), jnp.int32),
+            pltpu.VMEM((blocks, edges, width), BF16),
+            pltpu.VMEM((blocks, edges, width), BF16),
+            pltpu.VMEM((blocks, edges, width), BF16),
+            pltpu.VMEM((n_rep, blocks, edges), F32),
+            pltpu.VMEM((blocks, edges), F32),
+            pltpu.VMEM((stops, blocks, edges), F32),
+            pltpu.VMEM((stops, negs // 2, width), BF16),
+            pltpu.VMEM((negs, dim), BF16),
+            pltpu.VMEM((n_rep * edges, dim), BF16),
+            pltpu.VMEM((rows, n_rep * edges), BF16),
+            pltpu.VMEM((n_rep - 1, rows, width), BF16),
+            pltpu.VMEM((n_rep - 1, rows, width), BF16),
+            pltpu.VMEM((n_rep, edges, dim), BF16),
+            pltpu.VMEM((stops, width), F32),
+            pltpu.VMEM((n_rep, 1, width), F32),
+            dma((n_blk // 2,)), dma((n_blk // 2,)), dma((n_blk // 2,)), dma((n_blk // 2,)),
+            dma((n_rep,)), dma((n_rep,)), dma((stops,)), dma((stops,)),
+            dma((n_rep,)), dma((n_rep,)), dma((stops,)), dma((stops,)),
+            dma((n_rep,)), dma((n_rep,)), dma, dma, dma((n_rep,)), dma((n_rep,)),
+        ],
+        compiler_params=pltpu.CompilerParams(
+            collective_id=0, has_side_effects=True, vmem_limit_bytes=48 * 1024 * 1024
+        ),
+    )(neg_owner, embeddings, relation, ids, neg_ids)
 
 
 def shifted(shard, axis, by):
@@ -31,7 +305,7 @@
     return (empty.at[head_index].add(head_terms), empty.at[context_index].add(context_terms))
 
 
-def per_device(embeddings, relation, head_ids, context_ids, neg_owner, neg_ids):
+def by_collectives(embeddings, relation, head_ids, context_ids, neg_owner, neg_ids):
     weight = 4.0 / neg_ids.shape[1]
     stop_count = head_ids.shape[0]
     visitor = embeddings
@@ -59,9 +333,18 @@
     return lax.psum_scatter(combined, "rep", scatter_dimension=1, tiled=True)
 
 
+def per_device(n_blk, n_rep, embeddings, relation, head_ids, context_ids, neg_owner, neg_ids):
+    rows, dim = embeddings.shape
+    stops = head_ids.shape[0]
+    fits = n_blk * rows * (dim // n_rep) * 2 <= 8 * 1024 * 1024
+    if fits and n_rep == stops and n_blk > stops and n_blk % 2 == 0:
+        return fused(n_blk, n_rep, embeddings, relation, head_ids, context_ids, neg_owner, neg_ids)
+    return by_collectives(embeddings, relation, head_ids, context_ids, neg_owner, neg_ids)
+
+
 def solution(mesh):
     in_specs = (P("blk", None), P(), P(None, ("blk", "rep")), P(None, ("blk", "rep")), P(), P())
     out_specs = P("blk", "rep")
     return jax.shard_map(
-        per_device, mesh=mesh, in_specs=in_specs, out_specs=out_specs, check_vma=False
+        functools.partial(per_device, mesh.shape["blk"], mesh.shape["rep"]), mesh=mesh, in_specs=in_specs, out_specs=out_specs, check_vma=False
     )

time: 246 us -> 71.9 us (0.29); the launches traced: 241 us -> 71.6 us
  waiting for transfers between devices: 135 us -> 0 us
  Pallas kernels: 0 us -> 68.2 us
  other arithmetic: 40.5 us -> 0.74 us
  local copies, waits for them, and re-layouts: 31.6 us -> 2.72 us
  between operations: 16.5 us -> 0.02 us
  starting transfers between devices: 10.1 us -> 0 us
  matrix products: 7.54 us -> 0 us
    pallas_call x0 -> x1, Pallas kernels: none -> 68.2 us  [fused(): pl.pallas_call(functools.partial(kernel, n_blk, n_rep, 4.0 / negs), out_s...]
    reduce_scatter x1 -> x0, waiting for transfers between devices: 47.3 us -> none  [per_device(): return lax.psum_scatter(combined, 'rep', scatter_dimension=1, tiled=True)]
    ppermute x8 -> x0, waiting for transfers between devices: 44.5 us -> none  [shifted(): lax.ppermute(shard, axis, [(i, (i + by) % peers) for i in range(peers)])]
    psum x1 -> x0, waiting for transfers between devices: 43.1 us -> none  [broadcast(): return lax.psum(kept, axis)]
    gather x12 -> x0, local copies, waits for them, and re-layouts: 28.3 us -> none  [the longest x4 14.1 us: per_device(): picked = jnp.take(embeddings, neg_ids[stop_index], axis=0)]
    scatter-add x5 -> x0, other arithmetic: 16 us -> none  [the longest x4 12.4 us: stop_terms(): empty.at[context_index].add(context_terms)]
    add x2 -> x0, other arithmetic: 13.1 us -> none  [the longest x1 8.12 us: per_device(): head_total = head_total + head_part]
    ppermute x8 -> x0, starting transfers between devices: 10 us -> none  [shifted(): lax.ppermute(shard, axis, [(i, (i + by) % peers) for i in range(peers)])]
  transfers between devices with their start and end apart: 10 -> 0, of which waited for: 5 -> 0; matrix products, arithmetic and copies ran while one was open for 31% -> 0% of each run, Pallas kernels for 0% -> 0%
where the time goes in v1:
time: 71.9 us; the launch traced here: 71.6 us
  Pallas kernels  68.2 us (95%)
  local copies, waits for them, and re-layouts  2.72 us (4%)
  other arithmetic  0.74 us (1%)
    pallas_call x1, Pallas kernels, fused(): pl.pallas_call(functools.partial(kernel, n_blk, n_rep, 4.0 / negs), out_s...  68.2 us
    unnamed x9, local copies, waits for them, and re-layouts  2.72 us

profile of v1, /device:TPU:11, one launch (start us, length us, event | category | flops | bytes accessed | tf_op | source)
XLA Modules:
  0.0 71.6 jit_solution(11479077058589078611)
XLA Ops:
  0.0 0.0 copy-start.1
  0.0 0.0 copy-start.3
  0.0 0.7 %pad_add_fusion.ids_ref = s32[8,256]{1,0:T(8,128)S(1)} fusion(s32[4,256]{1,0:T(4,128)} %param.9, s32[4,256]{1,0:T(4,128)} %param.8), kind=kLoop, calls=%fused_computation | loop fusion | flops 2048 | bytes 16384 | tf_op jit(solution)/shard_map/concatenate | solution.py:242
  0.7 0.0 copy-done.1
  0.7 0.0 copy-done.3
  0.7 0.0 copy-start
  0.8 1.2 %copy-done = bf16[1024,512]{1,0:T(8,128)(2,1)S(1)} copy-done((bf16[1024,512]{1,0:T(8,128)(2,1)S(1)}, bf16[1024,512]{1,0:T(8,128)(2,1)}, u32[]{:S(2)}) %copy-start) | copy-done | bytes 1048600
  2.0 0.0 copy-start.2
  2.0 0.7 copy-done.2
  2.7 68.2 %shard_map.64 = f32[1024,128]{1,0:T(8,128)S(1)} custom-call(s32[4]{0:T(128)S(1)} %copy-done.3, bf16[1024,512]{1,0:T(8,128)(2,1)S(1)} %copy-done, f32[4,512]{1,0:T(4,128)S(1)} %copy-done.2, s32[8,256]{1,0:T(8,128)S(1)} %pad_add_fusion.ids_ref, s32[4,768]{1,0:T(4,128)S(1)} %copy-done.1), custom_call_target="tpu_custom_call" | custom-call | tf_op jit(solution)/shard_map/pallas_call | solution.py:246
  70.8 0.8 %copy.8 = f32[1024,128]{1,0:T(8,128)} copy(f32[1024,128]{1,0:T(8,128)S(1)} %shard_map.64) | data formatting | bytes 1048576
Async XLA Ops:
  0.0 0.7 %copy-start.1 = (s32[4,768]{1,0:T(4,128)S(1)}, s32[4,768]{1,0:T(4,128)}, u32[]{:S(2)}) copy-start(s32[4,768]{1,0:T(4,128)} %neg_ids_ref.1) | copy-start | bytes 36868
  0.0 0.7 %copy-start.3 = (s32[4]{0:T(128)S(1)}, s32[4]{0:T(128)}, u32[]{:S(2)}) copy-start(s32[4]{0:T(128)} %owner_ref.1) | copy-start | bytes 52
  0.7 1.2 %copy-start = (bf16[1024,512]{1,0:T(8,128)(2,1)S(1)}, bf16[1024,512]{1,0:T(8,128)(2,1)}, u32[]{:S(2)}) copy-start(bf16[1024,512]{1,0:T(8,128)(2,1)} %emb_ref.1) | copy-start | bytes 3145732
  2.0 0.7 copy-start.2

commit v2 on v1

v2 whole, which is shorter than its diff:
```python
import functools

import jax
import jax.numpy as jnp
from jax import lax
from jax.experimental import pallas as pl
from jax.experimental.pallas import tpu as pltpu
from jax.sharding import PartitionSpec as P

MESH = pl.DeviceIdType.MESH
F32 = jnp.float32
BF16 = jnp.bfloat16


def column_of(row):
    wide = jnp.broadcast_to(row.astype(F32), (8, row.shape[1]))
    return jnp.transpose(wide)[:, :1]


def by_edge(row, rows):
    column = column_of(row)
    lanes = lax.broadcasted_iota(jnp.int32, (row.shape[1], rows), 1).astype(F32)
    return jnp.where(column == lanes, 1.0, 0.0).astype(BF16)


def by_entity(row, rows, value):
    sublanes = lax.broadcasted_iota(jnp.int32, (rows, row.shape[1]), 0)
    return jnp.where(row == sublanes, value, 0.0).astype(BF16)


def kernel(
    n_blk, n_rep, weight,
    owner_ref, emb_hbm, rel_hbm, head_hbm, ctx_hbm, negid_hbm, out_ref,
    emb, rel, neg_ids, load_sem,
    parts, idz, idn, mine, his, ctx, part_dot, pos_grad, pos_in, neg_hot, neg_cut, neg, pulled, spread, give, take,
    wide, rel_wide, ag_send, ag_recv, fw_send, fw_recv, idz_send, idz_recv, idn_send, idn_recv,
    dot_send, dot_recv, pg_send, pg_recv, neg_send, neg_recv, sib_send, sib_recv, rs_send, rs_recv,
):
    b, z = lax.axis_index("blk"), lax.axis_index("rep")
    rows = emb.shape[0]
    stops = rel.shape[0]
    edges = idz.shape[2]
    width = out_ref.shape[1]
    half = neg_ids.shape[1] // 2
    core = lax.rem(b, 2)
    sibling = b + 1 - 2 * core
    cols = pl.ds(pl.multiple_of(z * width, width), width)
    inner = (z >= 1) & (z <= 2)
    first_stop = jnp.where(z == 2, 2, 0)

    def plane(j):
        return lax.rem(b + j + n_blk, n_blk)

    def column_peer(j):
        return lax.rem(z + j + n_rep, n_rep)

    def remote(src, dst, send, recv, at_blk, at_rep):
        return pltpu.make_async_remote_copy(
            src_ref=src, dst_ref=dst, send_sem=send, recv_sem=recv,
            device_id=(at_blk, at_rep), device_id_type=MESH,
        )

    barrier = pltpu.get_barrier_semaphore()
    for j in range(1, n_blk):
        pl.semaphore_signal(barrier, inc=1, device_id=(plane(j), z), device_id_type=MESH)
    for j in range(1, n_rep):
        pl.semaphore_signal(barrier, inc=1, device_id=(b, column_peer(j)), device_id_type=MESH)
    loads = [
        pltpu.make_async_copy(emb_hbm, emb, load_sem.at[0]),
        pltpu.make_async_copy(head_hbm, idz.at[z, pl.ds(0, stops)], load_sem.at[1]),
        pltpu.make_async_copy(ctx_hbm, idz.at[z, pl.ds(stops, stops)], load_sem.at[2]),
        pltpu.make_async_copy(rel_hbm, rel, load_sem.at[3]),
        pltpu.make_async_copy(negid_hbm, neg_ids, load_sem.at[4]),
    ]
    for copy in loads:
        copy.start()
    for copy in loads[1:]:
        copy.wait()
    loads[0].wait()
    parts[b] = jnp.transpose(emb[:, cols])
    pl.semaphore_wait(barrier, n_blk - 1 + n_rep - 1)

    jumps = list(range(2, n_blk, 2))
    ag_copies = [
        remote(parts.at[b], parts.at[b], ag_send.at[i], ag_recv.at[i], plane(j), z)
        for i, j in enumerate(jumps)
    ]
    for copy in ag_copies:
        copy.start()
    own_fw = remote(parts.at[b], parts.at[b], fw_send.at[len(jumps)], fw_recv.at[len(jumps)], sibling, z)
    own_fw.start()
    idz_copies = [
        remote(idz.at[z], idz.at[z], idz_send.at[j], idz_recv.at[j], b, column_peer(j))
        for j in range(1, n_rep)
    ]
    for copy in idz_copies:
        copy.start()

    rel_cols = rel[:, cols]
    for s in range(stops):
        rel_wide[s] = jnp.broadcast_to(column_of(rel_cols[s : s + 1, :]), (width, edges))
    for s in range(stops):
        ids_row = jnp.where(core == 0, neg_ids[s : s + 1, :half], neg_ids[s : s + 1, half:])
        neg_hot[s] = by_edge(ids_row, rows)

    for copy in idz_copies:
        copy.wait()
    idn_copies = [
        remote(idz, idn.at[k - 1], idn_send.at[k - 1], idn_recv.at[k - 1], plane(-k), z)
        for k in range(1, stops + 1)
    ]
    for copy in idn_copies:
        copy.start()

    def gather_wide(i, carry):
        s = first_stop + i
        for r in range(n_rep):
            at = pl.ds(pl.multiple_of((i * n_rep + r) * edges, edges), edges)
            ids_row = idz[r, pl.ds(s, 1), :]
            picked = jnp.dot(by_edge(ids_row, rows), emb[...], preferred_element_type=F32)
            wide[at, :] = (picked * rel[pl.ds(s, 1), :]).astype(BF16)
            spread[:, at] = by_entity(ids_row, rows, 1.0)
        return carry

    @pl.when(inner)
    def _():
        lax.fori_loop(0, 2, gather_wide, 0)

    fw_copies = []
    for i, j in enumerate(jumps):
        ag_copies[i].wait()
        source = plane(-j)
        copy = remote(parts.at[source], parts.at[source], fw_send.at[i], fw_recv.at[i], sibling, z)
        copy.start()
        fw_copies.append(copy)

    def gather_home(s, carry):
        for r in range(n_rep):
            hot = by_entity(idz[r, pl.ds(s, 1), :], rows, 1.0)
            picked = jnp.dot(parts[b], hot, preferred_element_type=F32)
            mine[s * n_rep + r] = (picked * rel_wide[s]).astype(BF16)
        return carry

    lax.fori_loop(0, stops, gather_home, 0)
    for copy in fw_copies + [own_fw]:
        copy.wait()

    lower = pl.ds(pl.multiple_of(core * half, half), half)
    by_row = (((1,), (1,)), ((), ()))
    neg_copies = []
    for s in range(stops):
        cut = lax.dot_general(neg_hot[s], parts[owner_ref[s]], by_row, preferred_element_type=F32)
        neg_cut[s] = cut.astype(BF16)
        to = 1 + s // 2
        copy = remote(
            neg_cut.at[s], neg.at[s % 2, lower, cols], neg_send.at[s], neg_recv.at[s % 2, z], b, to
        )
        neg_copies.append((to, copy))

        @pl.when(z != to)
        def _():
            copy.start()

        @pl.when(z == to)
        def _():
            neg[s % 2, lower, cols] = neg_cut[s]

    def gather_context(s, carry):
        source = lax.rem(b - s - 1 + n_blk, n_blk)
        for r in range(n_rep):
            t = s * n_rep + r
            hot = by_entity(idz[r, pl.ds(stops + s, 1), :], rows, 1.0)
            rows_in = jnp.dot(parts[source], hot, preferred_element_type=F32)
            ctx[t] = rows_in.astype(BF16)
            product = mine[t].astype(F32) * rows_in
            part_dot[z, pl.ds(t, 1), :] = jnp.sum(product, axis=0, keepdims=True)
        return carry

    lax.fori_loop(0, stops, gather_context, 0)
    dot_copies = [
        remote(part_dot.at[z], part_dot.at[z], dot_send.at[j], dot_recv.at[j], b, column_peer(j))
        for j in range(1, n_rep)
    ]
    for copy in dot_copies:
        copy.start()
    for copy in idn_copies:
        copy.wait()

    def gather_incoming(s, carry):
        source = lax.rem(b + s + 1, n_blk)
        for r in range(n_rep):
            hot = by_entity(idn[s, r, pl.ds(s, 1), :], rows, 1.0)
            picked = jnp.dot(parts[source], hot, preferred_element_type=F32)
            his[s * n_rep + r] = (picked * rel_wide[s]).astype(BF16)
        return carry

    for to, copy in neg_copies:

        @pl.when(z != to)
        def _():
            copy.wait_send()

    sib_copy = remote(neg.at[:, lower, :], neg.at[:, lower, :], sib_send, sib_recv, sibling, z)

    @pl.when(inner)
    def _():
        for i in range(2):
            for source in range(n_rep):

                @pl.when(z != source)
                def _():
                    there = pl.ds(source * width, width)
                    remote(
                        neg_cut.at[i], neg.at[i, lower, there], neg_send.at[i], neg_recv.at[i, source], b, source
                    ).wait_recv()

        sib_copy.start()

    for copy in dot_copies:
        copy.wait()
    positive = part_dot[0]
    for r in range(1, n_rep):
        positive = positive + part_dot[r]
    pos_grad[...] = -jax.nn.sigmoid(-positive)
    pg_copies = [
        remote(pos_grad, pos_in.at[k - 1], pg_send.at[k - 1], pg_recv.at[k - 1], plane(-k), z)
        for k in range(1, stops + 1)
    ]
    for copy in pg_copies:
        copy.start()

    def negatives(t, carry):
        i = t // n_rep
        at = pl.ds(pl.multiple_of(t * edges, edges), edges)
        scores = lax.dot_general(wide[at, :], neg[i], by_row, preferred_element_type=F32)
        neg_grad = (weight * jax.nn.sigmoid(scores)).astype(BF16)
        pull = jnp.dot(neg_grad, neg[i], preferred_element_type=F32)
        pulled[at, :] = (pull * rel[pl.ds(first_stop + i, 1), :]).astype(BF16)
        return carry

    def rs_copy(to):
        return remote(give.at[to], take.at[z - 1], rs_send.at[to], rs_recv.at[z - 1], b, to)

    @pl.when(inner)
    def _():
        sib_copy.wait()
        lax.fori_loop(0, 2 * n_rep, negatives, 0)
        for to in (0, 3, 1, 2):
            there = pl.ds(to * width, width)
            summed = jnp.dot(spread[...], pulled[:, there], preferred_element_type=F32)
            give[to] = summed.astype(BF16)

            @pl.when(z != to)
            def _():
                rs_copy(to).start()

            @pl.when(z == to)
            def _():
                out_ref[...] = summed

    @pl.when(jnp.logical_not(inner))
    def _():
        out_ref[...] = jnp.zeros_like(out_ref)

    lax.fori_loop(0, stops, gather_incoming, 0)

    def scatter_home(s, carry):
        total = jnp.zeros((rows, width), F32)
        for r in range(n_rep):
            t = s * n_rep + r
            hot = by_entity(idz[r, pl.ds(s, 1), :], rows, pos_grad[pl.ds(t, 1), :])
            rows_in = (ctx[t].astype(F32) * rel_wide[s]).astype(BF16)
            total = total + lax.dot_general(hot, rows_in, by_row, preferred_element_type=F32)
        out_ref[...] += total
        return carry

    lax.fori_loop(0, stops, scatter_home, 0)
    for copy in pg_copies:
        copy.wait()

    def scatter_incoming(s, carry):
        total = jnp.zeros((rows, width), F32)
        for r in range(n_rep):
            t = s * n_rep + r
            hot = by_entity(idn[s, r, pl.ds(stops + s, 1), :], rows, pos_in[s, pl.ds(t, 1), :])
            total = total + lax.dot_general(hot, his[t], by_row, preferred_element_type=F32)
        out_ref[...] += total
        return carry

    lax.fori_loop(0, stops, scatter_incoming, 0)
    for source in (1, 2):

        @pl.when(z != source)
        def _():
            remote(
                give.at[0], take.at[source - 1], rs_send.at[0], rs_recv.at[source - 1], b, source
            ).wait_recv()
            out_ref[...] += take[source - 1].astype(F32)

    @pl.when(inner)
    def _():
        for to in range(n_rep):

            @pl.when(z != to)
            def _():
                rs_copy(to).wait_send()


def fused(n_blk, n_rep, embeddings, relation, head_ids, context_ids, neg_owner, neg_ids):
    rows, dim = embeddings.shape
    stops, edges = head_ids.shape
    negs = neg_ids.shape[1]
    width = dim // n_rep
    blocks = stops * n_rep
    hbm = pl.BlockSpec(memory_space=pl.ANY)
    dma = pltpu.SemaphoreType.DMA
    return pl.pallas_call(
        functools.partial(kernel, n_blk, n_rep, 4.0 / negs),
        out_shape=jax.ShapeDtypeStruct((rows, width), F32),
        in_specs=[pl.BlockSpec(memory_space=pltpu.SMEM)] + [hbm] * 5,
        out_specs=pl.BlockSpec(memory_space=pltpu.VMEM),
        scratch_shapes=[
            pltpu.VMEM((rows, dim), BF16),
            pltpu.VMEM((stops, dim), F32),
            pltpu.VMEM((stops, negs), jnp.int32),
            dma((5,)),
            pltpu.VMEM((n_blk, width, rows), BF16),
            pltpu.VMEM((n_rep, 2 * stops, edges), jnp.int32),
            pltpu.VMEM((stops, n_rep, 2 * stops, edges), jnp.int32),
            pltpu.VMEM((blocks, width, edges), BF16),
            pltpu.VMEM((blocks, width, edges), BF16),
            pltpu.VMEM((blocks, width, edges), BF16),
            pltpu.VMEM((n_rep, blocks, edges), F32),
            pltpu.VMEM((blocks, edges), F32),
            pltpu.VMEM((stops, blocks, edges), F32),
            pltpu.VMEM((stops, negs // 2, rows), BF16),
            pltpu.VMEM((stops, negs // 2, width), BF16),
            pltpu.VMEM((2, negs, dim), BF16),
            pltpu.VMEM((2 * n_rep * edges, dim), BF16),
            pltpu.VMEM((rows, 2 * n_rep * edges), BF16),
            pltpu.VMEM((n_rep, rows, width), BF16),
            pltpu.VMEM((2, rows, width), BF16),
            pltpu.VMEM((2 * n_rep * edges, dim), BF16),
            pltpu.VMEM((stops, width, edges), F32),
            dma((n_blk // 2,)), dma((n_blk // 2,)), dma((n_blk // 2,)), dma((n_blk // 2,)),
            dma((n_rep,)), dma((n_rep,)), dma((stops,)), dma((stops,)),
            dma((n_rep,)), dma((n_rep,)), dma((stops,)), dma((stops,)),
            dma((stops,)), dma((2, n_rep)), dma, dma, dma((n_rep,)), dma((2,)),
        ],
        compiler_params=pltpu.CompilerParams(
            collective_id=0, has_side_effects=True, vmem_limit_bytes=52 * 1024 * 1024
        ),
    )(neg_owner, embeddings, relation, head_ids, context_ids, neg_ids)


def shifted(shard, axis, by):
    peers = lax.axis_size(axis)
    return lax.ppermute(shard, axis, [(i, (i + by) % peers) for i in range(peers)])


def broadcast(value, axis, source):
    kept = jnp.where(lax.axis_index(axis) == source, value, 0).astype(value.dtype)
    return lax.psum(kept, axis)


def stop_terms(home_rows, visitor, negatives, relation_row, head_index, context_index, weight):
    head_rows = jnp.take(home_rows, head_index, axis=0)
    context_rows = jnp.take(visitor, context_index, axis=0)
    weighted = (head_rows.astype(jnp.float32) * relation_row).astype(jnp.bfloat16)
    positive = jnp.sum(weighted.astype(jnp.float32) * context_rows.astype(jnp.float32), axis=1)
    scores = lax.dot_general(
        weighted, negatives, (((1,), (1,)), ((), ())), preferred_element_type=jnp.float32
    )
    pos_grad = -jax.nn.sigmoid(-positive)
    neg_grad = (weight * jax.nn.sigmoid(scores)).astype(jnp.bfloat16)
    pulled = jnp.dot(neg_grad, negatives, preferred_element_type=jnp.float32)
    head_terms = relation_row * (pos_grad[:, None] * context_rows.astype(jnp.float32) + pulled)
    context_terms = pos_grad[:, None] * weighted.astype(jnp.float32)
    empty = jnp.zeros((home_rows.shape[0], home_rows.shape[1]), jnp.float32)
    return (empty.at[head_index].add(head_terms), empty.at[context_index].add(context_terms))


def by_collectives(embeddings, relation, head_ids, context_ids, neg_owner, neg_ids):
    weight = 4.0 / neg_ids.shape[1]
    stop_count = head_ids.shape[0]
    visitor = embeddings
    head_total = jnp.zeros(embeddings.shape, jnp.float32)
    returned = jnp.zeros(embeddings.shape, jnp.float32)
    for stop_index in range(stop_count):
        visitor = shifted(visitor, "blk", 1)
        owner = neg_owner[stop_index]
        picked = jnp.take(embeddings, neg_ids[stop_index], axis=0)
        negatives = broadcast(picked, "blk", owner)
        head_part, context_part = stop_terms(
            embeddings,
            visitor,
            negatives,
            relation[stop_index],
            head_ids[stop_index],
            context_ids[stop_index],
            weight,
        )
        head_total = head_total + head_part
        returned = returned + shifted(
            context_part.astype(jnp.bfloat16), "blk", -(stop_index + 1)
        ).astype(context_part.dtype)
    combined = head_total + returned
    return lax.psum_scatter(combined, "rep", scatter_dimension=1, tiled=True)


def per_device(n_blk, n_rep, embeddings, relation, head_ids, context_ids, neg_owner, neg_ids):
    rows, dim = embeddings.shape
    stops = head_ids.shape[0]
    fits = n_blk * rows * (dim // n_rep) * 2 <= 8 * 1024 * 1024
    if fits and n_rep == stops == 4 and n_blk > stops and n_blk % 2 == 0:
        return fused(n_blk, n_rep, embeddings, relation, head_ids, context_ids, neg_owner, neg_ids)
    return by_collectives(embeddings, relation, head_ids, context_ids, neg_owner, neg_ids)


def solution(mesh):
    in_specs = (P("blk", None), P(), P(None, ("blk", "rep")), P(None, ("blk", "rep")), P(), P())
    out_specs = P("blk", "rep")
    return jax.shard_map(
        functools.partial(per_device, mesh.shape["blk"], mesh.shape["rep"]), mesh=mesh, in_specs=in_specs, out_specs=out_specs, check_vma=False
    )
```

time: 71.9 us -> 63.3 us (0.88); the launches traced: 71.6 us -> 62.1 us
  Pallas kernels: 68.2 us -> 56.6 us
  local copies, waits for them, and re-layouts: 2.72 us -> 5.45 us
  other arithmetic: 0.74 us -> 0 us
    pallas_call x1, Pallas kernels: 68.2 us -> 56.6 us  [fused(): pl.pallas_call(functools.partial(kernel, n_blk, n_rep, 4.0 / negs), out_s...]
    unnamed x9 -> x13, local copies, waits for them, and re-layouts: 2.72 us -> 5.45 us
    concatenate x1 -> x0, other arithmetic: 0.74 us -> none  [fused(): ids = jnp.concatenate([head_ids, context_ids], axis=0)]
where the time goes in v2:
time: 63.3 us; the launch traced here: 62.1 us
  Pallas kernels  56.6 us (89%)
  local copies, waits for them, and re-layouts  5.45 us (9%)
    pallas_call x1, Pallas kernels, fused(): pl.pallas_call(functools.partial(kernel, n_blk, n_rep, 4.0 / negs), out_s...  56.6 us
    unnamed x13, local copies, waits for them, and re-layouts  5.45 us

profile of v2, /device:TPU:11, one launch (start us, length us, event | category | flops | bytes accessed | tf_op | source)
XLA Modules:
  0.0 62.1 jit_solution(3387677978468576825)
XLA Ops:
  0.0 0.0 copy-start
  0.0 1.2 %copy-done = bf16[1024,512]{1,0:T(8,128)(2,1)S(1)} copy-done((bf16[1024,512]{1,0:T(8,128)(2,1)S(1)}, bf16[1024,512]{1,0:T(8,128)(2,1)}, u32[]{:S(2)}) %copy-start) | copy-done | bytes 1048600
  1.2 0.0 copy-start.1
  1.2 0.7 %copy-done.1 = s32[4,768]{1,0:T(4,128)S(1)} copy-done((s32[4,768]{1,0:T(4,128)S(1)}, s32[4,768]{1,0:T(4,128)}, u32[]{:S(2)}) %copy-start.1) | copy-done | bytes 12312
  1.9 0.0 copy-start.2
  1.9 0.7 %copy-done.2 = f32[4,512]{1,0:T(4,128)S(1)} copy-done((f32[4,512]{1,0:T(4,128)S(1)}, f32[4,512]{1,0:T(4,128)}, u32[]{:S(2)}) %copy-start.2) | copy-done | bytes 8216
  2.6 0.0 copy-start.3
  2.6 0.7 %copy-done.3 = s32[4,256]{1,0:T(4,128)S(1)} copy-done((s32[4,256]{1,0:T(4,128)S(1)}, s32[4,256]{1,0:T(4,128)}, u32[]{:S(2)}) %copy-start.3) | copy-done | bytes 4120
  3.3 0.0 copy-start.4
  3.3 0.7 %copy-done.4 = s32[4,256]{1,0:T(4,128)S(1)} copy-done((s32[4,256]{1,0:T(4,128)S(1)}, s32[4,256]{1,0:T(4,128)}, u32[]{:S(2)}) %copy-start.4) | copy-done | bytes 4120
  4.0 0.0 copy-start.5
  4.0 0.7 %copy-done.5 = s32[4]{0:T(128)S(1)} copy-done((s32[4]{0:T(128)S(1)}, s32[4]{0:T(128)}, u32[]{:S(2)}) %copy-start.5) | copy-done | bytes 40
  4.7 56.6 %shard_map.64 = f32[1024,128]{1,0:T(8,128)S(1)} custom-call(s32[4]{0:T(128)S(1)} %copy-done.5, bf16[1024,512]{1,0:T(8,128)(2,1)S(1)} %copy-done, f32[4,512]{1,0:T(4,128)S(1)} %copy-done.2, s32[4,256]{1,0:T(4,128)S(1)} %copy-done.3, s32[4,256]{1,0:T(4,128)S(1)} %copy-done.4, s32[4,768]{1,0:T(4,128)S(1)} %copy-done.1), custom_call_target="tpu_custom_call" | custom-call | tf_op jit(solution)/shard_map/pallas_call | solution.py:317
  61.3 0.8 %copy.8 = f32[1024,128]{1,0:T(8,128)} copy(f32[1024,128]{1,0:T(8,128)S(1)} %shard_map.64) | data formatting | bytes 1048576
Async XLA Ops:
  0.0 1.2 %copy-start = (bf16[1024,512]{1,0:T(8,128)(2,1)S(1)}, bf16[1024,512]{1,0:T(8,128)(2,1)}, u32[]{:S(2)}) copy-start(bf16[1024,512]{1,0:T(8,128)(2,1)} %emb_hbm.1) | copy-start | bytes 3145732
  1.2 0.7 %copy-start.1 = (s32[4,768]{1,0:T(4,128)S(1)}, s32[4,768]{1,0:T(4,128)}, u32[]{:S(2)}) copy-start(s32[4,768]{1,0:T(4,128)} %negid_hbm.1) | copy-start | bytes 36868
  1.9 0.7 %copy-start.2 = (f32[4,512]{1,0:T(4,128)S(1)}, f32[4,512]{1,0:T(4,128)}, u32[]{:S(2)}) copy-start(f32[4,512]{1,0:T(4,128)} %rel_hbm.1) | copy-start | bytes 24580
  2.6 0.7 %copy-start.3 = (s32[4,256]{1,0:T(4,128)S(1)}, s32[4,256]{1,0:T(4,128)}, u32[]{:S(2)}) copy-start(s32[4,256]{1,0:T(4,128)} %head_hbm.1) | copy-start | bytes 12292
  3.3 0.7 %copy-start.4 = (s32[4,256]{1,0:T(4,128)S(1)}, s32[4,256]{1,0:T(4,128)}, u32[]{:S(2)}) copy-start(s32[4,256]{1,0:T(4,128)} %ctx_hbm.1) | copy-start | bytes 12292
  4.0 0.7 %copy-start.5 = (s32[4]{0:T(128)S(1)}, s32[4]{0:T(128)}, u32[]{:S(2)}) copy-start(s32[4]{0:T(128)} %owner_ref.1) | copy-start | bytes 52

commit v3 on v2

--- a/solution.py
+++ b/solution.py
@@ -238,25 +238,33 @@
         pulled[at, :] = (pull * rel[pl.ds(first_stop + i, 1), :]).astype(BF16)
         return carry
 
-    def rs_copy(to):
-        return remote(give.at[to], take.at[z - 1], rs_send.at[to], rs_recv.at[z - 1], b, to)
+    cuts = rs_recv.shape[1]
+    cut_rows = rows // cuts
+
+    def rs_copy(to, cut):
+        at = pl.ds(cut * cut_rows, cut_rows)
+        return remote(
+            give.at[to, at], take.at[z - 1, at], rs_send.at[to, cut], rs_recv.at[z - 1, cut], b, to
+        )
 
     @pl.when(inner)
     def _():
         sib_copy.wait()
         lax.fori_loop(0, 2 * n_rep, negatives, 0)
-        for to in (0, 3, 1, 2):
-            there = pl.ds(to * width, width)
-            summed = jnp.dot(spread[...], pulled[:, there], preferred_element_type=F32)
-            give[to] = summed.astype(BF16)
-
-            @pl.when(z != to)
-            def _():
-                rs_copy(to).start()
-
-            @pl.when(z == to)
-            def _():
-                out_ref[...] = summed
+        for cut in range(cuts):
+            at = pl.ds(cut * cut_rows, cut_rows)
+            summed = jnp.dot(spread[at, :], pulled[...], preferred_element_type=F32)
+            for to in (0, 3, 1, 2):
+                chunk = summed[:, to * width : (to + 1) * width]
+                give[to, at, :] = chunk.astype(BF16)
+
+                @pl.when(z != to)
+                def _():
+                    rs_copy(to, cut).start()
+
+                @pl.when(z == to)
+                def _():
+                    out_ref[at, :] = chunk
 
     @pl.when(jnp.logical_not(inner))
     def _():
@@ -292,9 +300,12 @@
 
         @pl.when(z != source)
         def _():
-            remote(
-                give.at[0], take.at[source - 1], rs_send.at[0], rs_recv.at[source - 1], b, source
-            ).wait_recv()
+            for cut in range(cuts):
+                at = pl.ds(cut * cut_rows, cut_rows)
+                remote(
+                    give.at[0, at], take.at[source - 1, at], rs_send.at[0, cut], rs_recv.at[source - 1, cut],
+                    b, source,
+                ).wait_recv()
             out_ref[...] += take[source - 1].astype(F32)
 
     @pl.when(inner)
@@ -303,7 +314,8 @@
 
             @pl.when(z != to)
             def _():
-                rs_copy(to).wait_send()
+                for cut in range(cuts):
+                    rs_copy(to, cut).wait_send()
 
 
 def fused(n_blk, n_rep, embeddings, relation, head_ids, context_ids, neg_owner, neg_ids):
@@ -345,7 +357,7 @@
             dma((n_blk // 2,)), dma((n_blk // 2,)), dma((n_blk // 2,)), dma((n_blk // 2,)),
             dma((n_rep,)), dma((n_rep,)), dma((stops,)), dma((stops,)),
             dma((n_rep,)), dma((n_rep,)), dma((stops,)), dma((stops,)),
-            dma((stops,)), dma((2, n_rep)), dma, dma, dma((n_rep,)), dma((2,)),
+            dma((stops,)), dma((2, n_rep)), dma, dma, dma((n_rep, 4)), dma((2, 4)),
         ],
         compiler_params=pltpu.CompilerParams(
             collective_id=0, has_side_effects=True, vmem_limit_bytes=52 * 1024 * 1024

time: 63.3 us -> 60.8 us (0.961); the launches traced: 62.1 us -> 60.4 us
  Pallas kernels: 56.6 us -> 54.9 us
    pallas_call x1, Pallas kernels: 56.6 us -> 54.9 us  [fused(): pl.pallas_call(functools.partial(kernel, n_blk, n_rep, 4.0 / negs), out_s...]
where the time goes in v3:
time: 60.8 us; the launch traced here: 60.4 us
  Pallas kernels  54.9 us (90%)
  local copies, waits for them, and re-layouts  5.45 us (9%)
    pallas_call x1, Pallas kernels, fused(): pl.pallas_call(functools.partial(kernel, n_blk, n_rep, 4.0 / negs), out_s...  54.9 us
    unnamed x13, local copies, waits for them, and re-layouts  5.45 us

profile of v3, /device:TPU:11, one launch (start us, length us, event | category | flops | bytes accessed | tf_op | source)
XLA Modules:
  0.0 60.4 jit_solution(15433362715236109843)
XLA Ops:
  0.0 0.0 copy-start
  0.0 1.2 %copy-done = bf16[1024,512]{1,0:T(8,128)(2,1)S(1)} copy-done((bf16[1024,512]{1,0:T(8,128)(2,1)S(1)}, bf16[1024,512]{1,0:T(8,128)(2,1)}, u32[]{:S(2)}) %copy-start) | copy-done | bytes 1048600
  1.2 0.0 copy-start.1
  1.2 0.7 %copy-done.1 = s32[4,768]{1,0:T(4,128)S(1)} copy-done((s32[4,768]{1,0:T(4,128)S(1)}, s32[4,768]{1,0:T(4,128)}, u32[]{:S(2)}) %copy-start.1) | copy-done | bytes 12312
  1.9 0.0 copy-start.2
  1.9 0.7 %copy-done.2 = f32[4,512]{1,0:T(4,128)S(1)} copy-done((f32[4,512]{1,0:T(4,128)S(1)}, f32[4,512]{1,0:T(4,128)}, u32[]{:S(2)}) %copy-start.2) | copy-done | bytes 8216
  2.6 0.0 copy-start.3
  2.6 0.7 %copy-done.3 = s32[4,256]{1,0:T(4,128)S(1)} copy-done((s32[4,256]{1,0:T(4,128)S(1)}, s32[4,256]{1,0:T(4,128)}, u32[]{:S(2)}) %copy-start.3) | copy-done | bytes 4120
  3.3 0.0 copy-start.4
  3.3 0.7 %copy-done.4 = s32[4,256]{1,0:T(4,128)S(1)} copy-done((s32[4,256]{1,0:T(4,128)S(1)}, s32[4,256]{1,0:T(4,128)}, u32[]{:S(2)}) %copy-start.4) | copy-done | bytes 4120
  4.0 0.0 copy-start.5
  4.0 0.7 %copy-done.5 = s32[4]{0:T(128)S(1)} copy-done((s32[4]{0:T(128)S(1)}, s32[4]{0:T(128)}, u32[]{:S(2)}) %copy-start.5) | copy-done | bytes 40
  4.7 54.9 %shard_map.64 = f32[1024,128]{1,0:T(8,128)S(1)} custom-call(s32[4]{0:T(128)S(1)} %copy-done.5, bf16[1024,512]{1,0:T(8,128)(2,1)S(1)} %copy-done, f32[4,512]{1,0:T(4,128)S(1)} %copy-done.2, s32[4,256]{1,0:T(4,128)S(1)} %copy-done.3, s32[4,256]{1,0:T(4,128)S(1)} %copy-done.4, s32[4,768]{1,0:T(4,128)S(1)} %copy-done.1), custom_call_target="tpu_custom_call" | custom-call | tf_op jit(solution)/shard_map/pallas_call | solution.py:329
  59.6 0.8 %copy.8 = f32[1024,128]{1,0:T(8,128)} copy(f32[1024,128]{1,0:T(8,128)S(1)} %shard_map.64) | data formatting | bytes 1048576
Async XLA Ops:
  0.0 1.2 %copy-start = (bf16[1024,512]{1,0:T(8,128)(2,1)S(1)}, bf16[1024,512]{1,0:T(8,128)(2,1)}, u32[]{:S(2)}) copy-start(bf16[1024,512]{1,0:T(8,128)(2,1)} %emb_hbm.1) | copy-start | bytes 3145732
  1.2 0.7 %copy-start.1 = (s32[4,768]{1,0:T(4,128)S(1)}, s32[4,768]{1,0:T(4,128)}, u32[]{:S(2)}) copy-start(s32[4,768]{1,0:T(4,128)} %negid_hbm.1) | copy-start | bytes 36868
  1.9 0.7 %copy-start.2 = (f32[4,512]{1,0:T(4,128)S(1)}, f32[4,512]{1,0:T(4,128)}, u32[]{:S(2)}) copy-start(f32[4,512]{1,0:T(4,128)} %rel_hbm.1) | copy-start | bytes 24580
  2.6 0.7 %copy-start.3 = (s32[4,256]{1,0:T(4,128)S(1)}, s32[4,256]{1,0:T(4,128)}, u32[]{:S(2)}) copy-start(s32[4,256]{1,0:T(4,128)} %head_hbm.1) | copy-start | bytes 12292
  3.3 0.7 %copy-start.4 = (s32[4,256]{1,0:T(4,128)S(1)}, s32[4,256]{1,0:T(4,128)}, u32[]{:S(2)}) copy-start(s32[4,256]{1,0:T(4,128)} %ctx_hbm.1) | copy-start | bytes 12292
  4.0 0.7 %copy-start.5 = (s32[4]{0:T(128)S(1)}, s32[4]{0:T(128)}, u32[]{:S(2)}) copy-start(s32[4]{0:T(128)} %owner_ref.1) | copy-start | bytes 52
